TPU v7x, 32 devices: a whole 2x2x4 slice. The times are simulated.
32 devices in a mesh: grp: 2 (over y), aux: 16 (over z, x, core).
Axes of the slice: x: 2, y: 2, z: 4, core: 2. Of those that a mesh axis runs over, the one named last changes fastest.
Arguments:
- three_index: bfloat16 [160, 1024, 1024], P(('grp', 'aux')), parts along dimension 0, may hold values from -6 to 6
- screen: int32 [160, 256], P(('grp', 'aux')), parts along dimension 0, may hold values from 0 to 1, as said below
- orbitals: bfloat16 [2048, 16], P('grp'), parts along dimension 0, may hold values from -1 to 1
- fitting: bfloat16 [160, 80], P(('grp', 'aux')), parts along dimension 0, may hold values from -1 to 1
Outputs:
- exchange_matrix: float32 [2048, 1024], P(('grp', 'aux')), parts along dimension 0
There are 2 independent parts, one for each index of `grp`. A program takes and returns all parts, laid end to end along the dimension named above; each array names one. Nothing has to cross between parts.
Inputs may be any that keep to these rules, and one draw needn't show every extreme that they name: screen[P, a * 16 + a] is 1 for every P and a.
All inputs are finite; a program needn't handle non-finite values.
Results may differ from a plain program's by a relative error of at most 0.0026.
Values may be sent and summed in bfloat16 or wider, within the bound.
A program may use at most 128 MiB of HBM per device.

v0:
```python
import jax
import jax.numpy as jnp
from jax import lax
from jax.sharding import PartitionSpec as P


def fit_rows(rows_piece, flat_half):
    return jnp.dot(rows_piece, flat_half, preferred_element_type=jnp.float32).astype(jnp.bfloat16)


def shards(three_index, screen, orbitals, fitting):
    aux_count = lax.axis_size("aux")
    aux_rows, basis_count, unused = three_index.shape
    block_count = basis_count // 64
    orb_total = orbitals.shape[1]
    orb_dev = orb_total // aux_count
    total_aux = fitting.shape[1]
    screen_full = screen.reshape(aux_rows, block_count, 1, block_count, 1).astype(jnp.bfloat16)
    screen_full = jnp.broadcast_to(screen_full, (aux_rows, block_count, 64, block_count, 64))
    screened = three_index * screen_full.reshape(aux_rows, basis_count, basis_count)
    half_done = jnp.einsum(
        "pmn,ni->pmi", screened, orbitals, preferred_element_type=jnp.float32
    ).astype(jnp.bfloat16)
    half_done = half_done.reshape(aux_rows, basis_count, aux_count, orb_dev)
    regrouped = lax.all_to_all(half_done, "aux", split_axis=2, concat_axis=0, tiled=True)
    flat_half = regrouped.reshape(total_aux, basis_count * orb_dev)
    rows_piece = lax.all_gather(fitting, "aux", axis=0, tiled=True)
    fitted = fit_rows(rows_piece, flat_half).reshape(rows_piece.shape[0], basis_count, orb_dev)
    partial_value = lax.dot_general(
        fitted, fitted, (((0, 2), (0, 2)), ((), ())), preferred_element_type=jnp.float32
    )
    return lax.psum_scatter(partial_value, "aux", scatter_dimension=0, tiled=True)


def solution(mesh):
    return jax.shard_map(
        shards,
        mesh=mesh,
        in_specs=(
            P(("grp", "aux"), None, None),
            P(("grp", "aux"), None),
            P("grp", None),
            P(("grp", "aux"), None),
        ),
        out_specs=P(("grp", "aux"), None),
        check_vma=False,
    )
```

profile of v0, /device:TPU:0, one launch (start us, length us, event | category | flops | bytes accessed | tf_op | source)
XLA Modules:
  0.0 162.3 jit_solution(14366402219267567874)
XLA Ops:
  6.5 0.0 copy-start
  6.5 0.7 convert_element_type.18
  7.2 0.1 convert_element_type.19
  7.3 7.4 %broadcast_in_dim.2 = bf16[5,16,64,16,64]{4,3,2,1,0:T(8,128)(2,1)} broadcast(bf16[5,16,16]{2,1,0:T(8,128)(2,1)S(1)} %convert_element_type.19), dimensions={0,1,3} | broadcast | bytes 10488320 | tf_op jit(solution)/shard_map/broadcast_in_dim | solution.py:19
  14.7 28.0 %reshape.24 = bf16[5,1024,1024]{2,1,0:T(8,128)(2,1)} reshape(bf16[5,16,64,16,64]{4,3,2,1,0:T(8,128)(2,1)} %broadcast_in_dim.2) | data formatting | bytes 20971520 | tf_op jit(solution)/shard_map/reshape | solution.py:20
  42.7 0.0 copy-done
  42.7 0.0 copy-start.1
  42.7 9.8 %fusion.6 = bf16[5,1024,16,1]{1,2,0,3:T(8,128)(2,1)S(1)} fusion(bf16[5,1024,1024]{2,1,0:T(8,128)(2,1)} %param.4, bf16[5,1024,1024]{2,1,0:T(8,128)(2,1)} %reshape.24, bf16[1024,16]{0,1:T(8,128)(2,1)S(1)} %copy-done), kind=kOutput, calls=%fused_computation.5 | convolution fusion | flops 173096960 | bytes 21168128 | tf_op jit(solution)/shard_map/pmn,ni->pmi/dot_general | solution.py:21
  52.5 0.8 copy.6
  53.3 7.4 %all-to-all-start = ((bf16[5,1024,16,1]{1,0,3,2:T(8,128)(2,1)}), bf16[5,1024,16,1]{1,0,3,2:T(8,128)(2,1)S(1)}, u32[]{:S(2)}, u32[]{:S(2)}) async-start(bf16[5,1024,16,1]{1,0,3,2:T(8,128)(2,1)} %copy.6), calls=%async_computation | async-start | bytes 524288 | tf_op jit(solution)/shard_map/all_to_all | solution.py:25
  60.7 0.0 reduce-scatter.2.cloned.1.call-start
  60.7 0.0 copy-done.1
  60.7 21.9 %all-gather = bf16[16,5,80]{2,1,0:T(8,128)(2,1)S(1)} all-gather(bf16[1,5,80]{2,1,0:T(8,128)(2,1)S(1)} %bitcast.16), channel_id=1, replica_groups=mesh['grp'=2,'aux'=16] {'aux'}, dimensions={0}, use_global_device_ids=true | all-gather | bytes 13600 | tf_op jit(solution)/shard_map/all_gather | solution.py:27
  82.6 0.0 all-to-all-done
  82.7 0.1 reshape.26
  82.7 2.8 %fusion.2 = f32[1024,1024]{1,0:T(8,128)} fusion(bf16[80,80]{1,0:T(8,128)(2,1)S(1)} %reshape.28, bf16[80,1024]{1,0:T(8,128)(2,1)S(1)} %reshape.26), kind=kOutput, calls=%fused_computation.3 | convolution fusion | flops 180961280 | bytes 4370944 | tf_op jit(solution)/shard_map/dot_general | solution.py:29
  85.6 0.0 reduce-scatter.2.cloned.1.call-update
  85.6 69.9 %reduce-scatter.2.cloned.1.call-done = f32[64,1024]{1,0:T(8,128)} async-done(((f32[1024,1024]{1,0:T(8,128)}), f32[64,1024]{1,0:T(8,128)}) %reduce-scatter.2.cloned.1.call-update) | async-done | bytes 262160 | tf_op jit(solution)/shard_map/reduce_scatter | solution.py:32
  (1 shorter events, 0.0 us)
Async XLA Ops:
  6.5 36.2 %copy-start = (bf16[1024,16]{0,1:T(8,128)(2,1)S(1)}, bf16[1024,16]{0,1:T(8,128)(2,1)}, u32[]{:S(2)}) copy-start(bf16[1024,16]{0,1:T(8,128)(2,1)} %param.6) | copy-start | bytes 98308
  42.7 18.0 %copy-start.1 = (bf16[5,80]{1,0:T(8,128)(2,1)S(1)}, bf16[5,80]{1,0:T(8,128)(2,1)}, u32[]{:S(2)}) copy-start(bf16[5,80]{1,0:T(8,128)(2,1)} %param.7) | copy-start | bytes 2404
  53.3 29.3 %all-to-all-start = ((bf16[5,1024,16,1]{1,0,3,2:T(8,128)(2,1)}), bf16[5,1024,16,1]{1,0,3,2:T(8,128)(2,1)S(1)}, u32[]{:S(2)}, u32[]{:S(2)}) async-start(bf16[5,1024,16,1]{1,0,3,2:T(8,128)(2,1)} %copy.6), calls=%async_computation | async-start | bytes 524288 | tf_op jit(solution)/shard_map/all_to_all | solution.py:25
  60.7 94.8 %reduce-scatter.2.cloned.1.call-start = ((), (), s32[]{:S(2)}) async-start(), calls=%async_computation.2 | async-start | bytes 4456448 | tf_op jit(solution)/shard_map/reduce_scatter | solution.py:32
Sparse Core Ops, SparseCore 0:
  85.7 69.7 reduce-scatter.1
where the time goes:
time: 163 us; the launch traced here: 162 us
  waiting for transfers between devices  69.9 us (43%)
  local copies, waits for them, and re-layouts  36.4 us (22%)
  blocking collectives  21.9 us (13%)
  between operations  13.4 us (8%)
  matrix products  12.6 us (8%)
  starting transfers between devices  7.4 us (5%)
    reduce_scatter x1, waiting for transfers between devices, shards(): lax.psum_scatter(partial_value, 'aux', scatter_dimension=0, tiled=True)  69.9 us
    reshape x1, local copies, waits for them, and re-layouts, shards(): screen_full.reshape(aux_rows, basis_count, basis_count)  28 us
    all_gather x1, blocking collectives, shards(): rows_piece = lax.all_gather(fitting, 'aux', axis=0, tiled=True)  21.9 us
    dot_general x1, matrix products, shards(): jnp.einsum('pmn,ni->pmi', screened, orbitals, preferred_element_type=jnp....  9.79 us
    broadcast_in_dim x1, local copies, waits for them, and re-layouts, shards(): jnp.broadcast_to(screen_full, (aux_rows, block_count, 64, block_count, 64))  7.36 us
    all_to_all x1, starting transfers between devices, shards(): lax.all_to_all(half_done, 'aux', split_axis=2, concat_axis=0, tiled=True)  7.36 us
  transfers between devices with their start and end apart: 2, of which 1 were waited for; matrix products, arithmetic and copies ran while one was open for 0% of the time, Pallas kernels for 0%

commit v1 on v0

v1 whole, which is shorter than its diff:
```python
import functools

import jax
import jax.numpy as jnp
from jax import lax
from jax.experimental import pallas as pl
from jax.experimental.pallas import tpu as pltpu
from jax.sharding import PartitionSpec as P

BF = jnp.bfloat16
F32 = jnp.float32
BLK = 64
CHUNK = 256


def iota(shape, dim):
    return lax.broadcasted_iota(jnp.int32, shape, dim)


def kernel(cfg, t_hbm, screen_hbm, orb_hbm, fit_hbm, out_ref, tbuf, screen_v, orb_v, fit_v, wbuf, mbuf, gath,
           fall, kron, ft_s, y_s, t_sem, in_sem, fsend, frecv, send_sem, recv_sem):
    devs, rows, basis, occ, total = cfg
    chunks = basis // CHUNK
    nblk = basis // BLK
    slab = rows * occ
    zs = devs // 4
    me = lax.axis_index("aux")
    z, core = me // 4, me % 2
    xn = me + 2 - 4 * ((me // 2) % 2)
    sib = me + 1 - 2 * core

    small = [
        pltpu.make_async_copy(screen_hbm, screen_v, in_sem.at[0]),
        pltpu.make_async_copy(orb_hbm, orb_v, in_sem.at[1]),
        pltpu.make_async_copy(fit_hbm, fit_v, in_sem.at[2]),
    ]
    for copy in small:
        copy.start()

    def t_copy(k, p):
        part = pl.ds(k * CHUNK, CHUNK)
        return pltpu.make_async_copy(t_hbm.at[p, part], tbuf.at[p, part], t_sem.at[k, p])

    for k in range(chunks):
        for p in range(rows):
            t_copy(k, p).start()

    barrier = pltpu.get_barrier_semaphore()

    @pl.loop(1, devs)
    def _(off):
        pl.semaphore_signal(barrier, inc=1, device_id={"aux": lax.rem(me + off, devs)})

    small[0].wait()
    spread = jnp.where(iota((nblk * nblk, basis), 0) % nblk == iota((nblk * nblk, basis), 1) // BLK, 1.0, 0.0).astype(BF)
    own = iota((16 * nblk, nblk * nblk), 0) // 16 == iota((16 * nblk, nblk * nblk), 1) // nblk
    for p in range(rows):
        marks = jnp.where(own, screen_v[pl.ds(p, 1), :].astype(F32), 0.0).astype(BF)
        mbuf[p] = jnp.dot(marks, spread, preferred_element_type=F32).astype(BF)
    small[1].wait()
    for p in range(rows):
        shift = jnp.where(iota((occ, 128), 0) + occ * p == iota((occ, 128), 1), 1.0, 0.0).astype(BF)
        wbuf[p] = jnp.dot(orb_v[...], shift, preferred_element_type=F32).astype(BF)
    small[2].wait()
    fall[me] = jnp.zeros((16, 128), BF)
    fall[me, pl.ds(0, rows), pl.ds(0, total)] = fit_v[...]

    pl.semaphore_wait(barrier, devs - 1)

    def fit_copy(off):
        return pltpu.make_async_remote_copy(
            src_ref=fall.at[me], dst_ref=fall.at[me], send_sem=fsend.at[off], recv_sem=frecv.at[me],
            device_id={"aux": lax.rem(me + off, devs)})

    @pl.loop(1, devs)
    def _(off):
        fit_copy(off).start()

    def copy(o, k, way, target):
        part = gath.at[k, pl.ds(pl.multiple_of(o * slab, 16), slab), :]
        return pltpu.make_async_remote_copy(
            src_ref=part, dst_ref=part, send_sem=send_sem.at[way, o, k], recv_sem=recv_sem.at[o, k],
            device_id={"aux": target})

    def arrive(o, k):
        copy(o, k, 0, sib).wait_recv()

    def up(o, k, act):
        @pl.when(z < zs - 1)
        def _():
            act(copy(o, k, 0, lax.rem(me + 4, devs)))

    def down(o, k, act):
        @pl.when(z > 0)
        def _():
            act(copy(o, k, 1, lax.rem(me + devs - 4, devs)))

    def across(o, k, act):
        act(copy(o, k, 2, xn))

    def beside(o, k, act):
        act(copy(o, k, 3, sib))

    start = lambda c: c.start()
    finish = lambda c: c.wait_send()

    @pl.loop(0, chunks)
    def _(k):
        total_rows = pl.ds(pl.multiple_of(k * CHUNK, CHUNK), CHUNK)
        acc = jnp.zeros((CHUNK, 128), F32)
        for p in range(rows):
            t_copy(k, p).wait()
            marks = mbuf[p, pl.ds(pl.multiple_of(k * (CHUNK // BLK * 16), 16), CHUNK // BLK * 16), :]
            marks = marks.reshape(CHUNK // BLK, 1, 16, basis)
            lhs = tbuf[p, total_rows, :].reshape(CHUNK // BLK, BLK // 16, 16, basis) * marks
            acc += jnp.dot(lhs.reshape(CHUNK, basis), wbuf[p], preferred_element_type=F32)
        half = jnp.transpose(acc)[:slab].astype(BF)
        gath[k, pl.ds(pl.multiple_of(me * slab, 16), slab), :] = half
        up(me, k, start)
        down(me, k, start)
        across(me, k, start)
        beside(me, k, start)

    def build_kron():
        @pl.loop(1, devs)
        def _(off):
            o = lax.rem(me + off, devs)
            pltpu.make_async_remote_copy(
                src_ref=fall.at[o], dst_ref=fall.at[o], send_sem=fsend.at[off], recv_sem=frecv.at[o],
                device_id={"aux": o}).wait_recv()

        wide = jnp.where(iota((128, devs * slab), 0) == iota((128, devs * slab), 1) // occ, 1.0, 0.0).astype(BF)
        flat = jnp.dot(fall[...].reshape(devs * 16, 128), wide, preferred_element_type=F32).astype(BF)

        @pl.loop(0, devs * slab // 256)
        def _(b):
            q = (iota((256, devs * 16), 0) + b * 256) // occ
            col = iota((256, devs * 16), 1)
            pick = jnp.where((q // rows) * 16 + q % rows == col, 1.0, 0.0).astype(BF)
            full = jnp.dot(pick, flat, preferred_element_type=F32)
            same = iota((256, devs * slab), 0) % occ == iota((256, devs * slab), 1) % occ
            kron[pl.ds(pl.multiple_of(b * 256, 256), 256), :] = jnp.where(same, full, 0.0).astype(BF)

    def each(s, base, act):
        @pl.when(z >= s)
        def _():
            act(lax.rem(base + devs - 4 * s, devs), True)

        if s > 0:
            @pl.when(z + s < zs)
            def _():
                act(lax.rem(base + 4 * s, devs), False)

    for s in range(1, zs + 1):
        @pl.loop(0, chunks)
        def _(k):
            if s < zs:
                def line(o, rising):
                    arrive(o, k)
                    (up if rising else down)(o, k, start)
                    across(o, k, start)
                    beside(o, k, start)
                each(s, me, line)

            def side(o, rising):
                arrive(o, k)
                beside(o, k, start)
            each(s - 1, xn, side)

        if s == 1:
            build_kron()

    @pl.loop(0, devs // 2)
    def _(h):
        for k in range(chunks):
            arrive(2 * h + 1 - core, k)

    per = out_ref.shape[0]
    first = me * per
    lane = pl.multiple_of((first % CHUNK) // 128 * 128, 128)
    mine = gath[first // CHUNK, :, pl.ds(lane, 128)]
    fitted = jnp.dot(kron[...], mine, preferred_element_type=F32)
    ft_s[...] = jnp.transpose(fitted)
    mine_t = ft_s[pl.ds(pl.multiple_of(first % 128, 8), per), :].astype(BF)
    y = jnp.dot(mine_t, kron[...], preferred_element_type=F32)
    high = y.astype(BF)
    y_s[:per] = high
    y_s[per:] = (y - high.astype(F32)).astype(BF)
    for k in range(chunks):
        both = jnp.dot(y_s[...], gath[k], preferred_element_type=F32)
        out_ref[:, k * CHUNK:(k + 1) * CHUNK] = both[:per] + both[per:]

    @pl.loop(0, chunks)
    def _(k):
        up(me, k, finish)
        down(me, k, finish)
        across(me, k, finish)
        beside(me, k, finish)
        for s in range(1, zs + 1):
            if s < zs:
                def line(o, rising):
                    (up if rising else down)(o, k, finish)
                    across(o, k, finish)
                    beside(o, k, finish)
                each(s, me, line)

            def side(o, rising):
                beside(o, k, finish)
            each(s - 1, xn, side)

    @pl.loop(1, devs)
    def _(off):
        fit_copy(off).wait_send()


def gathered(three_index, screen, orbitals, fitting):
    devs = lax.axis_size("aux")
    rows, basis, _ = three_index.shape
    occ = orbitals.shape[1]
    total = fitting.shape[1]
    slab = rows * occ
    chunks = basis // CHUNK
    anywhere = pl.BlockSpec(memory_space=pl.ANY)
    dma = pltpu.SemaphoreType.DMA
    return pl.pallas_call(
        functools.partial(kernel, (devs, rows, basis, occ, total)),
        out_shape=jax.ShapeDtypeStruct((basis // devs, basis), F32),
        in_specs=[anywhere] * 4,
        out_specs=pl.BlockSpec(memory_space=pltpu.VMEM),
        scratch_shapes=[
            pltpu.VMEM(three_index.shape, BF),
            pltpu.VMEM(screen.shape, jnp.int32),
            pltpu.VMEM(orbitals.shape, BF),
            pltpu.VMEM(fitting.shape, BF),
            pltpu.VMEM((rows, basis, 128), BF),
            pltpu.VMEM((rows, 16 * basis // BLK, basis), BF),
            pltpu.VMEM((chunks, devs * slab, CHUNK), BF),
            pltpu.VMEM((devs, 16, 128), BF),
            pltpu.VMEM((devs * slab, devs * slab), BF),
            pltpu.VMEM((128, devs * slab), F32),
            pltpu.VMEM((2 * basis // devs, devs * slab), BF),
            dma((chunks, rows)),
            dma((3,)),
            dma((devs,)),
            dma((devs,)),
            dma((4, devs, chunks)),
            dma((devs, chunks)),
        ],
        compiler_params=pltpu.CompilerParams(
            collective_id=0, has_side_effects=True, vmem_limit_bytes=48 * 1024 * 1024),
        cost_estimate=pl.CostEstimate(
            flops=2 * rows * basis * basis * occ, bytes_accessed=2 * rows * basis * basis, transcendentals=0),
    )(three_index, screen, orbitals, fitting)


def by_orbital(three_index, screen, orbitals, fitting):
    aux_count = lax.axis_size("aux")
    aux_rows, basis_count, _ = three_index.shape
    block_count = basis_count // BLK
    orb_dev = orbitals.shape[1] // aux_count
    total_aux = fitting.shape[1]
    screen_full = screen.reshape(aux_rows, block_count, 1, block_count, 1).astype(BF)
    screen_full = jnp.broadcast_to(screen_full, (aux_rows, block_count, BLK, block_count, BLK))
    screened = three_index * screen_full.reshape(aux_rows, basis_count, basis_count)
    half = jnp.einsum("pmn,ni->pmi", screened, orbitals, preferred_element_type=F32).astype(BF)
    half = half.reshape(aux_rows, basis_count, aux_count, orb_dev)
    half = lax.all_to_all(half, "aux", split_axis=2, concat_axis=0, tiled=True)
    flat = half.reshape(total_aux, basis_count * orb_dev)
    whole_fit = lax.all_gather(fitting, "aux", axis=0, tiled=True)
    fitted = jnp.dot(whole_fit, flat, preferred_element_type=F32).astype(BF)
    fitted = fitted.reshape(whole_fit.shape[0], basis_count, orb_dev)
    partial_value = lax.dot_general(fitted, fitted, (((0, 2), (0, 2)), ((), ())), preferred_element_type=F32)
    return lax.psum_scatter(partial_value, "aux", scatter_dimension=0, tiled=True)


def shards(three_index, screen, orbitals, fitting):
    devs = lax.axis_size("aux")
    rows, basis, _ = three_index.shape
    slab = rows * orbitals.shape[1]
    fits = (
        devs % 4 == 0 and slab <= 128 and slab % 16 == 0 and rows <= 16 and fitting.shape[1] <= 128
        and basis % CHUNK == 0 and (devs * slab) % 256 == 0 and 128 % (basis // devs) == 0
        and rows * basis * basis + (basis + devs * slab) * devs * slab <= 12 * 1024 * 1024
    )
    return (gathered if fits else by_orbital)(three_index, screen, orbitals, fitting)


def solution(mesh):
    return jax.shard_map(
        shards,
        mesh=mesh,
        in_specs=(
            P(("grp", "aux"), None, None),
            P(("grp", "aux"), None),
            P("grp", None),
            P(("grp", "aux"), None),
        ),
        out_specs=P(("grp", "aux"), None),
        check_vma=False,
    )
```

time: 163 us -> 37.7 us (0.23)
  the two profiles are of different devices: /device:TPU:0 before, /device:TPU:1 now
where the time goes in v1:
time: 37.7 us; the launch traced here: 37.5 us
  Pallas kernels  34.4 us (91%)
  local copies, waits for them, and re-layouts  3 us (8%)
    pallas_call x1, Pallas kernels, gathered(): pl.pallas_call(functools.partial(kernel, (devs, rows, basis, occ, total))...  34.4 us
    unnamed x6, local copies, waits for them, and re-layouts  3 us

profile of v1, /device:TPU:1, one launch (start us, length us, event | category | flops | bytes accessed | tf_op | source)
XLA Modules:
  0.0 37.5 jit_solution(4847437270854882760)
XLA Ops:
  0.0 0.9 %copy.5.orb_hbm = bf16[1024,16]{1,0:T(8,128)(2,1)S(1)} copy(bf16[1024,16]{0,1:T(8,128)(2,1)} %param.6) | data formatting | bytes 65536 | tf_op args[2]
  0.9 0.0 copy-start
  0.9 0.7 %copy-done = s32[5,256]{1,0:T(8,128)S(1)} copy-done((s32[5,256]{1,0:T(8,128)S(1)}, s32[5,256]{1,0:T(8,128)}, u32[]{:S(2)}) %copy-start) | copy-done | bytes 5144
  1.6 0.0 copy-start.1
  1.6 0.7 %copy-done.1 = bf16[5,80]{1,0:T(8,128)(2,1)S(1)} copy-done((bf16[5,80]{1,0:T(8,128)(2,1)S(1)}, bf16[5,80]{1,0:T(8,128)(2,1)}, u32[]{:S(2)}) %copy-start.1) | copy-done | bytes 824
  2.3 34.4 %shard_map.46 = f32[64,1024]{1,0:T(8,128)S(1)} custom-call(bf16[5,1024,1024]{2,1,0:T(8,128)(2,1)} %t_hbm.1, s32[5,256]{1,0:T(8,128)S(1)} %copy-done, bf16[1024,16]{1,0:T(8,128)(2,1)S(1)} %copy.5.orb_hbm, bf16[5,80]{1,0:T(8,128)(2,1)S(1)} %copy-done.1), custom_call_target="tpu_custom_call" | custom-call | flops 167772160 | bytes 10485760 | tf_op jit(solution)/shard_map/pallas_call | solution.py:225
  36.8 0.7 %copy.7 = f32[64,1024]{1,0:T(8,128)} copy(f32[64,1024]{1,0:T(8,128)S(1)} %shard_map.46) | data formatting | bytes 524288
Async XLA Ops:
  0.9 0.7 %copy-start = (s32[5,256]{1,0:T(8,128)S(1)}, s32[5,256]{1,0:T(8,128)}, u32[]{:S(2)}) copy-start(s32[5,256]{1,0:T(8,128)} %screen_hbm.1) | copy-start | bytes 15364
  1.6 0.7 %copy-start.1 = (bf16[5,80]{1,0:T(8,128)(2,1)S(1)}, bf16[5,80]{1,0:T(8,128)(2,1)}, u32[]{:S(2)}) copy-start(bf16[5,80]{1,0:T(8,128)(2,1)} %fit_hbm.1) | copy-start | bytes 2404

commit v2 on v1

--- a/solution.py
+++ b/solution.py
@@ -10,7 +10,9 @@
 BF = jnp.bfloat16
 F32 = jnp.float32
 BLK = 64
-CHUNK = 256
+CHUNK = 512
+CROSS = 0
+REV = False
 
 
 def iota(shape, dim):
@@ -18,7 +20,7 @@
 
 
 def kernel(cfg, t_hbm, screen_hbm, orb_hbm, fit_hbm, out_ref, tbuf, screen_v, orb_v, fit_v, wbuf, mbuf, gath,
-           fall, kron, ft_s, y_s, t_sem, in_sem, fsend, frecv, send_sem, recv_sem):
+           fall, fit_s, mine_s, ft_s, y_s, t_sem, in_sem, fsend, frecv, send_sem, recv_sem):
     devs, rows, basis, occ, total = cfg
     chunks = basis // CHUNK
     nblk = basis // BLK
@@ -60,7 +62,8 @@
     small[1].wait()
     for p in range(rows):
         shift = jnp.where(iota((occ, 128), 0) + occ * p == iota((occ, 128), 1), 1.0, 0.0).astype(BF)
-        wbuf[p] = jnp.dot(orb_v[...], shift, preferred_element_type=F32).astype(BF)
+        wbuf[p] = lax.dot_general(
+            orb_v[...], shift, (((0,), (0,)), ((), ())), preferred_element_type=F32).astype(BF)
     small[2].wait()
     fall[me] = jnp.zeros((16, 128), BF)
     fall[me, pl.ds(0, rows), pl.ds(0, total)] = fit_v[...]
@@ -121,7 +124,7 @@
         across(me, k, start)
         beside(me, k, start)
 
-    def build_kron():
+    def build_fit():
         @pl.loop(1, devs)
         def _(off):
             o = lax.rem(me + off, devs)
@@ -129,17 +132,9 @@
                 src_ref=fall.at[o], dst_ref=fall.at[o], send_sem=fsend.at[off], recv_sem=frecv.at[o],
                 device_id={"aux": o}).wait_recv()
 
-        wide = jnp.where(iota((128, devs * slab), 0) == iota((128, devs * slab), 1) // occ, 1.0, 0.0).astype(BF)
-        flat = jnp.dot(fall[...].reshape(devs * 16, 128), wide, preferred_element_type=F32).astype(BF)
-
-        @pl.loop(0, devs * slab // 256)
-        def _(b):
-            q = (iota((256, devs * 16), 0) + b * 256) // occ
-            col = iota((256, devs * 16), 1)
-            pick = jnp.where((q // rows) * 16 + q % rows == col, 1.0, 0.0).astype(BF)
-            full = jnp.dot(pick, flat, preferred_element_type=F32)
-            same = iota((256, devs * slab), 0) % occ == iota((256, devs * slab), 1) % occ
-            kron[pl.ds(pl.multiple_of(b * 256, 256), 256), :] = jnp.where(same, full, 0.0).astype(BF)
+        q, col = iota((total, devs * 16), 0), iota((total, devs * 16), 1)
+        pick = jnp.where((q // rows) * 16 + q % rows == col, 1.0, 0.0).astype(BF)
+        fit_s[...] = jnp.dot(pick, fall[...].reshape(devs * 16, 128), preferred_element_type=F32).astype(BF)
 
     def each(s, base, act):
         @pl.when(z >= s)
@@ -151,24 +146,37 @@
             def _():
                 act(lax.rem(base + 4 * s, devs), False)
 
+    def relay(s, k, act, waits):
+        late = k >= chunks - CROSS
+
+        def line(o, rising):
+            waits(o, k)
+            (up if rising else down)(o, k, act)
+            if not late:
+                across(o, k, act)
+            beside(o, k, act)
+
+        def side(o, rising):
+            waits(o, k)
+            if late and s == 1:
+                up(o, k, act)
+                down(o, k, act)
+            elif late:
+                (up if rising else down)(o, k, act)
+            beside(o, k, act)
+
+        if late:
+            each(s - 1, xn, side)
+        if s < zs:
+            each(s, me, line)
+        if not late:
+            each(s - 1, xn, side)
+
     for s in range(1, zs + 1):
-        @pl.loop(0, chunks)
-        def _(k):
-            if s < zs:
-                def line(o, rising):
-                    arrive(o, k)
-                    (up if rising else down)(o, k, start)
-                    across(o, k, start)
-                    beside(o, k, start)
-                each(s, me, line)
-
-            def side(o, rising):
-                arrive(o, k)
-                beside(o, k, start)
-            each(s - 1, xn, side)
-
+        for k in reversed(range(chunks)) if s == 1 and REV else range(chunks):
+            relay(s, k, start, arrive)
         if s == 1:
-            build_kron()
+            build_fit()
 
     @pl.loop(0, devs // 2)
     def _(h):
@@ -178,11 +186,14 @@
     per = out_ref.shape[0]
     first = me * per
     lane = pl.multiple_of((first % CHUNK) // 128 * 128, 128)
-    mine = gath[first // CHUNK, :, pl.ds(lane, 128)]
-    fitted = jnp.dot(kron[...], mine, preferred_element_type=F32)
-    ft_s[...] = jnp.transpose(fitted)
-    mine_t = ft_s[pl.ds(pl.multiple_of(first % 128, 8), per), :].astype(BF)
-    y = jnp.dot(mine_t, kron[...], preferred_element_type=F32)
+    mine_s[...] = gath[first // CHUNK, :, pl.ds(lane, 128)].astype(F32)
+    mine = jnp.concatenate([mine_s[pl.ds(i, total, occ), :].astype(BF) for i in range(occ)], axis=1)
+    fitted = jnp.dot(fit_s[:, :total], mine, preferred_element_type=F32).astype(BF)
+    back = lax.dot_general(fit_s[...], fitted, (((0,), (0,)), ((), ())), preferred_element_type=F32)
+    for i in range(occ):
+        mine_s[pl.ds(i, total, occ), :] = back[:total, i * 128:(i + 1) * 128]
+    ft_s[...] = jnp.transpose(mine_s[...])
+    y = ft_s[pl.ds(pl.multiple_of(first % 128, 8), per), :]
     high = y.astype(BF)
     y_s[:per] = high
     y_s[per:] = (y - high.astype(F32)).astype(BF)
@@ -190,23 +201,13 @@
         both = jnp.dot(y_s[...], gath[k], preferred_element_type=F32)
         out_ref[:, k * CHUNK:(k + 1) * CHUNK] = both[:per] + both[per:]
 
-    @pl.loop(0, chunks)
-    def _(k):
+    for k in range(chunks):
         up(me, k, finish)
         down(me, k, finish)
         across(me, k, finish)
         beside(me, k, finish)
         for s in range(1, zs + 1):
-            if s < zs:
-                def line(o, rising):
-                    (up if rising else down)(o, k, finish)
-                    across(o, k, finish)
-                    beside(o, k, finish)
-                each(s, me, line)
-
-            def side(o, rising):
-                beside(o, k, finish)
-            each(s - 1, xn, side)
+            relay(s, k, finish, lambda o, k: None)
 
     @pl.loop(1, devs)
     def _(off):
@@ -220,7 +221,7 @@
     total = fitting.shape[1]
     slab = rows * occ
     chunks = basis // CHUNK
-    anywhere = pl.BlockSpec(memory_space=pl.ANY)
+    anywhere = pl.BlockSpec(memory_space=pltpu.HBM)
     dma = pltpu.SemaphoreType.DMA
     return pl.pallas_call(
         functools.partial(kernel, (devs, rows, basis, occ, total)),
@@ -230,13 +231,14 @@
         scratch_shapes=[
             pltpu.VMEM(three_index.shape, BF),
             pltpu.VMEM(screen.shape, jnp.int32),
-            pltpu.VMEM(orbitals.shape, BF),
+            pltpu.VMEM((occ, basis), BF),
             pltpu.VMEM(fitting.shape, BF),
             pltpu.VMEM((rows, basis, 128), BF),
             pltpu.VMEM((rows, 16 * basis // BLK, basis), BF),
             pltpu.VMEM((chunks, devs * slab, CHUNK), BF),
             pltpu.VMEM((devs, 16, 128), BF),
-            pltpu.VMEM((devs * slab, devs * slab), BF),
+            pltpu.VMEM((total, 128), BF),
+            pltpu.VMEM((devs * slab, 128), F32),
             pltpu.VMEM((128, devs * slab), F32),
             pltpu.VMEM((2 * basis // devs, devs * slab), BF),
             dma((chunks, rows)),
@@ -247,10 +249,10 @@
             dma((devs, chunks)),
         ],
         compiler_params=pltpu.CompilerParams(
-            collective_id=0, has_side_effects=True, vmem_limit_bytes=48 * 1024 * 1024),
+            collective_id=0, has_side_effects=True, vmem_limit_bytes=62 * 1024 * 1024),
         cost_estimate=pl.CostEstimate(
             flops=2 * rows * basis * basis * occ, bytes_accessed=2 * rows * basis * basis, transcendentals=0),
-    )(three_index, screen, orbitals, fitting)
+    )(three_index, screen, orbitals.T, fitting)
 
 
 def by_orbital(three_index, screen, orbitals, fitting):
@@ -278,9 +280,9 @@
     rows, basis, _ = three_index.shape
     slab = rows * orbitals.shape[1]
     fits = (
-        devs % 4 == 0 and slab <= 128 and slab % 16 == 0 and rows <= 16 and fitting.shape[1] <= 128
+        devs % 4 == 0 and slab <= 128 and slab % 16 == 0 and rows <= 16 and fitting.shape[1] <= 128 and fitting.shape[1] == devs * rows
         and basis % CHUNK == 0 and (devs * slab) % 256 == 0 and 128 % (basis // devs) == 0
-        and rows * basis * basis + (basis + devs * slab) * devs * slab <= 12 * 1024 * 1024
+        and rows * basis * basis + basis * devs * slab <= 12 * 1024 * 1024
     )
     return (gathered if fits else by_orbital)(three_index, screen, orbitals, fitting)
 

time: 37.7 us -> 34.8 us (0.923)
  Pallas kernels: 34.4 us -> 33 us
  local copies, waits for them, and re-layouts: 3 us -> 1.67 us
    pallas_call x1, Pallas kernels: 34.4 us -> 33 us  [gathered(): pl.pallas_call(functools.partial(kernel, (devs, rows, basis, occ, total))...]
    unnamed x6 -> x1, local copies, waits for them, and re-layouts: 3 us -> 1.67 us
where the time goes in v2:
time: 34.8 us; the launch traced here: 34.7 us
  Pallas kernels  33 us (95%)
  local copies, waits for them, and re-layouts  1.67 us (5%)
    pallas_call x1, Pallas kernels, gathered(): pl.pallas_call(functools.partial(kernel, (devs, rows, basis, occ, total))...  33 us
    unnamed x1, local copies, waits for them, and re-layouts  1.67 us

profile of v2, /device:TPU:1, one launch (start us, length us, event | category | flops | bytes accessed | tf_op | source)
XLA Modules:
  0.0 34.7 jit_solution(12731738619862796337)
XLA Ops:
  0.0 33.0 %shard_map.46 = f32[64,1024]{1,0:T(8,128)} custom-call(bf16[5,1024,1024]{2,1,0:T(8,128)(2,1)} %t_hbm.1, s32[5,256]{1,0:T(8,128)} %screen_hbm.1, bf16[16,1024]{1,0:T(8,128)(2,1)} %bitcast.1, bf16[5,80]{1,0:T(8,128)(2,1)} %fit_hbm.1), custom_call_target="tpu_custom_call" | custom-call | flops 167772160 | bytes 10485760 | tf_op jit(solution)/shard_map/pallas_call | solution.py:226
  33.0 1.7 %copy.6 = f32[64,1024]{1,0:T(8,128)} copy(f32[64,1024]{1,0:T(8,128)} %shard_map.46) | data formatting | bytes 524288
